TPU v7x, 32 devices: a whole 2x2x4 slice. The times are simulated.
32 devices in a mesh: grp: 2 (over x), ref: 16 (over z, y, core).
Axes of the slice: x: 2, y: 2, z: 4, core: 2. Of those that a mesh axis runs over, the one named last changes fastest.
Arguments:
- references: bfloat16 [24576, 16384], P(('grp', 'ref')), parts along dimension 0
- noise: float32 [256, 16384], P('grp', 'ref'), parts along dimension 0
- init_idx: int32 [256], P('grp'), parts along dimension 0, may hold values from 0 to 12287
Outputs:
- paths: float32 [256, 16384], P('grp', 'ref'), parts along dimension 0
There are 2 independent parts, one for each index of `grp`. A program takes and returns all parts, laid end to end along the dimension named above; each array names one. Nothing has to cross between parts.
All inputs are finite; a program needn't handle non-finite values.
Results may differ from a plain program's by a relative error of at most 0.0003.
Values may be sent and summed in bfloat16 or wider, within the bound.
A program may use at most 128 MiB of HBM per device.

v0:
```python
import jax
import jax.numpy as jnp
from jax import lax
from jax.sharding import PartitionSpec as P

M = 128
STEPS = 2


SHARP = 7.0
STEP_RATE = 0.025


def shards(references, noise, init_idx):
    local_rows = references.shape[0]
    members = lax.axis_size("ref")
    position = lax.axis_index("ref")
    all_refs = local_rows * members
    ref_sq = jnp.sum(jnp.square(references.astype(jnp.float32)), axis=1)
    scale = lax.psum(jnp.sum(ref_sq), "ref") / all_refs
    offset = init_idx - position * local_rows
    owned = (offset >= 0) & (offset < local_rows)
    picked = references[jnp.clip(offset, 0, local_rows - 1)]
    picked = jnp.where(owned[:, None], picked, jnp.zeros_like(picked))
    seeded = lax.psum_scatter(
        picked.astype(jnp.float32).astype(jnp.bfloat16), "ref", scatter_dimension=1, tiled=True
    ).astype(jnp.float32)
    paths = 0.6 * seeded + 0.8 * noise
    count_paths = paths.shape[0]
    offdiag = 1.0 - jnp.eye(count_paths, dtype=jnp.float32)
    contract = (((1,), (1,)), ((), ()))
    for step in range(STEPS):
        pathb = paths.astype(jnp.bfloat16)
        piece = lax.all_gather(pathb, "ref", axis=1, tiled=True)
        new_scores = lax.dot_general(
            piece, references, contract, preferred_element_type=jnp.float32
        )
        new_gram = lax.dot_general(piece, piece, contract, preferred_element_type=jnp.float32)
        sq = jnp.diagonal(new_gram)
        weights = jnp.exp(
            SHARP * (2.0 * scale - sq[:, None] - ref_sq[None, :] + 2.0 * new_scores) / scale
        )
        totals = lax.psum(jnp.sum(weights, axis=1), "ref")
        weightb = weights.astype(jnp.bfloat16)
        pulled = lax.psum_scatter(
            lax.dot_general(
                references, weightb, (((0,), (1,)), ((), ())), preferred_element_type=jnp.float32
            ),
            "ref",
            scatter_dimension=0,
            tiled=True,
        ).T
        mutual = (
            jnp.exp(SHARP * (2.0 * scale - sq[:, None] - sq[None, :] + 2.0 * new_gram) / scale)
            * offdiag
        )
        mutual_sum = jnp.sum(mutual, axis=1)
        pushed = jnp.dot(mutual, paths, precision=lax.Precision.HIGHEST)
        paths = (
            paths
            + STEP_RATE / M * (mutual_sum[:, None] * paths - pushed)
            - STEP_RATE / all_refs * (totals[:, None] * paths - pulled)
        )
    return paths


def solution(mesh):
    in_specs = (P(("grp", "ref"), None), P("grp", "ref"), P("grp"))
    out_specs = P("grp", "ref")
    return jax.shard_map(shards, mesh=mesh, in_specs=in_specs, out_specs=out_specs, check_vma=False)
```

profile of v0, /device:TPU:0, one launch (start us, length us, event | category | flops | bytes accessed | tf_op | source)
XLA Modules:
  0.0 498.8 jit_solution(10807217915017659431)
XLA Ops:
  6.5 0.7 compare_select_fusion
  7.2 0.7 compare_and_fusion
  7.9 20.1 %gather_fusion = bf16[128,16384]{1,0:T(8,128)(2,1)} fusion(bf16[768,16384]{1,0:T(8,128)(2,1)} %param.3, s32[1024]{0:T(1024)S(1)} %pad_clamp_fusion), kind=kCustom, calls=%fused_computation | custom fusion | bytes 8389120 | tf_op jit(solution)/shard_map/gather | solution.py:23
  28.0 4.5 broadcast_select_fusion
  32.5 0.0 reduce-scatter.4.cloned.1.call-update
  32.5 0.0 all-gather.3.cloned.1.call-start
  32.5 75.2 %reduce-scatter.4.cloned.1.call-done = bf16[128,1024]{1,0:T(8,128)(2,1)} async-done(((bf16[128,16384]{1,0:T(8,128)(2,1)}), bf16[128,1024]{1,0:T(8,128)(2,1)}) %reduce-scatter.4.cloned.1.call-update) | async-done | bytes 262160 | tf_op jit(solution)/shard_map/reduce_scatter | solution.py:25
  107.7 1.7 fusion.18
  109.5 0.0 reduce-scatter.6.cloned.1.call-start
  109.5 16.4 %fusion = (f32[768]{0:T(1024)S(1)}, f32[]{:T(128)}) fusion(bf16[768,16384]{1,0:T(8,128)(2,1)} %param.3), kind=kLoop, calls=%fused_computation.4 | loop fusion | flops 50330880 | bytes 25168900 | tf_op jit(solution)/shard_map/reduce_sum | solution.py:19
  126.0 31.7 %psum.21 = f32[]{:T(128)} all-reduce(f32[]{:T(128)} %get-tuple-element.6), channel_id=1, replica_groups=mesh['grp'=2,'ref'=16] {'ref'}, use_global_device_ids=true, to_apply=%region_2.0 | all-reduce | flops 1 | bytes 8 | tf_op jit(solution)/shard_map/psum | solution.py:20
  158.9 0.6 all-gather.3.cloned.1.call-done
  159.5 4.7 fusion.32
  164.2 1.3 gather_fusion.1
  165.5 13.6 %fusion.29 = (f32[128]{0:T(128)S(1)}, bf16[128,768]{1,0:T(8,128)(2,1)S(1)}) fusion(f32[]{:T(128)S(6)} %div.23, bf16[128,16384]{1,0:T(8,128)(2,1)} %all-gather.3.cloned.1.call-done, bf16[768,16384]{1,0:T(8,128)(2,1)} %param.3, f32[768]{0:T(1024)S(1)} %get-tuple-element.5, f32[128]{0:T(128)S(1)} %broadcast_subtract_fusion.1), kind=kOutput, calls=%fused_computation.51 | convolution fusion | flops 3221913600 | bytes 29560836 | tf_op jit(solution)/shard_map/dot_general | solution.py:35
  179.2 14.9 %convolution_bitcast_fusion.1 = f32[16384,128]{0,1:T(8,128)} fusion(bf16[768,16384]{1,0:T(8,128)(2,1)} %param.3, bf16[128,768]{1,0:T(8,128)(2,1)S(1)} %get-tuple-element.8), kind=kOutput, calls=%fused_computation.7 | convolution fusion | flops 3221225472 | bytes 33751040 | tf_op jit(solution)/shard_map/dot_general | solution.py:46
  194.1 0.0 all-gather.5.cloned.1.call-start
  194.2 31.8 %psum.22 = f32[128]{0:T(128)S(1)} all-reduce(f32[128]{0:T(128)S(1)} %get-tuple-element.7), channel_id=1, replica_groups=mesh['grp'=2,'ref'=16] {'ref'}, use_global_device_ids=true, to_apply=%region_6.7 | all-reduce | flops 128 | bytes 1024 | tf_op jit(solution)/shard_map/psum | solution.py:43
  226.0 0.1 fusion.27
  226.1 72.2 %reduce-scatter.6.cloned.1.call-done = f32[1024,128]{0,1:T(8,128)} async-done(((f32[16384,128]{0,1:T(8,128)}), f32[1024,128]{0,1:T(8,128)}) %reduce-scatter.6.cloned.1.call-update) | async-done | bytes 524304 | tf_op jit(solution)/shard_map/reduce_scatter | solution.py:45
  298.3 2.6 fusion.30
  301.0 0.0 all-gather.5.cloned.1.call-update
  301.0 0.3 reduce-scatter.8.cloned.1.call-start
  301.3 50.2 %all-gather.5.cloned.1.call-done = bf16[128,16384]{1,0:T(8,128)(2,1)} async-done(((bf16[128,1024]{1,0:T(8,128)(2,1)}), bf16[128,16384]{1,0:T(8,128)(2,1)}) %all-gather.5.cloned.1.call-update) | async-done | bytes 4194320 | tf_op jit(solution)/shard_map/all_gather | solution.py:34
  351.5 4.7 fusion.33
  356.2 1.3 gather_fusion.2
  357.5 13.6 %fusion.31 = (f32[128]{0:T(128)S(1)}, bf16[128,768]{1,0:T(8,128)(2,1)S(1)}) fusion(f32[]{:T(128)S(6)} %div.23, bf16[128,16384]{1,0:T(8,128)(2,1)} %all-gather.5.cloned.1.call-done, bf16[768,16384]{1,0:T(8,128)(2,1)} %param.3, f32[768]{0:T(1024)S(1)} %get-tuple-element.5, f32[128]{0:T(128)S(1)} %broadcast_subtract_fusion), kind=kOutput, calls=%fused_computation.53 | convolution fusion | flops 3221913600 | bytes 29560836 | tf_op jit(solution)/shard_map/dot_general | solution.py:35
  371.2 14.9 %convolution_bitcast_fusion = f32[16384,128]{0,1:T(8,128)} fusion(bf16[768,16384]{1,0:T(8,128)(2,1)} %param.3, bf16[128,768]{1,0:T(8,128)(2,1)S(1)} %get-tuple-element.12), kind=kOutput, calls=%fused_computation.6 | convolution fusion | flops 3221225472 | bytes 33751040 | tf_op jit(solution)/shard_map/dot_general | solution.py:46
  386.1 31.1 %psum.23 = f32[128]{0:T(128)S(1)} all-reduce(f32[128]{0:T(128)S(1)} %get-tuple-element.11), channel_id=1, replica_groups=mesh['grp'=2,'ref'=16] {'ref'}, use_global_device_ids=true, to_apply=%region_10.11 | all-reduce | flops 128 | bytes 1024 | tf_op jit(solution)/shard_map/psum | solution.py:43
  417.3 0.1 fusion.28
  417.4 72.2 %reduce-scatter.8.cloned.1.call-done = f32[1024,128]{0,1:T(8,128)} async-done(((f32[16384,128]{0,1:T(8,128)}), f32[1024,128]{0,1:T(8,128)}) %reduce-scatter.8.cloned.1.call-update) | async-done | bytes 524304 | tf_op jit(solution)/shard_map/reduce_scatter | solution.py:45
  489.6 2.7 fusion.4
  (12 shorter events, 0.1 us)
Async XLA Ops:
  6.5 101.2 %reduce-scatter.4.cloned.1.call-start = ((), (), s32[]{:S(2)}) async-start(), calls=%async_computation.3 | async-start | bytes 4456448 | tf_op jit(solution)/shard_map/reduce_scatter | solution.py:25
  32.5 75.2 %copy-start = (f32[128,1024]{1,0:T(8,128)S(1)}, f32[128,1024]{1,0:T(8,128)}, u32[]{:S(2)}) copy-start(f32[128,1024]{1,0:T(8,128)} %param.4) | copy-start | bytes 1572868
  32.5 127.0 %all-gather.3.cloned.1.call-start = ((), (), s32[]{:S(2)}) async-start(), calls=%async_computation.4 | async-start | bytes 4456448 | tf_op jit(solution)/shard_map/all_gather | solution.py:34
  109.5 188.9 %reduce-scatter.6.cloned.1.call-start = ((), (), s32[]{:S(2)}) async-start(), calls=%async_computation.5 | async-start | bytes 8912896 | tf_op jit(solution)/shard_map/reduce_scatter | solution.py:45
  194.1 104.2 %copy-start.1 = (bf16[128,1024]{1,0:T(8,128)(2,1)S(1)}, bf16[128,1024]{1,0:T(8,128)(2,1)}, u32[]{:S(2)}) copy-start(bf16[128,1024]{1,0:T(8,128)(2,1)} %reduce-scatter.4.cloned.1.call-done) | copy-start | bytes 786436
  194.1 157.4 %all-gather.5.cloned.1.call-start = ((), (), s32[]{:S(2)}) async-start(), calls=%async_computation.6 | async-start | bytes 4456448 | tf_op jit(solution)/shard_map/all_gather | solution.py:34
  301.0 188.6 %reduce-scatter.8.cloned.1.call-start = ((), (), s32[]{:S(2)}) async-start(), calls=%async_computation.7 | async-start | bytes 8912896 | tf_op jit(solution)/shard_map/reduce_scatter | solution.py:45
Sparse Core Ops, SparseCore 0:
  32.6 75.0 reduce-scatter.3
  110.1 49.3 all-gather.2
  194.2 104.0 reduce-scatter.5
  301.1 50.3 all-gather.4
  386.2 103.3 reduce-scatter.7
where the time goes:
time: 499 us
  waiting for transfers between devices  271 us (54%)
  blocking collectives  94.7 us (19%)
  matrix products  71.9 us (14%)
  other arithmetic  24.2 us (5%)
  local copies, waits for them, and re-layouts  22.7 us (5%)
  between operations  14.4 us (3%)
    reduce_scatter x2, waiting for transfers between devices, shards(): lax.psum_scatter(lax.dot_general(references, weightb, (((0,), (1,)), ((),...  144 us
    reduce_scatter x1, waiting for transfers between devices, shards(): lax.psum_scatter(picked.astype(jnp.float32).astype(jnp.bfloat16), 'ref',...  75.2 us
    psum x2, blocking collectives, shards(): totals = lax.psum(jnp.sum(weights, axis=1), 'ref')  63 us
    all_gather x2, waiting for transfers between devices, shards(): piece = lax.all_gather(pathb, 'ref', axis=1, tiled=True)  50.8 us
    psum x1, blocking collectives, shards(): scale = lax.psum(jnp.sum(ref_sq), 'ref') / all_refs  31.7 us
    dot_general x2, matrix products, shards(): lax.dot_general(references, weightb, (((0,), (1,)), ((), ())), preferred_...  29.9 us
    dot_general x2, matrix products, shards(): lax.dot_general(piece, references, contract, preferred_element_type=jnp.f...  27.3 us
    gather x1, local copies, waits for them, and re-layouts, shards(): picked = references[jnp.clip(offset, 0, local_rows - 1)]  20.1 us
  transfers between devices with their start and end apart: 5, of which 5 were waited for; matrix products, arithmetic and copies ran while one was open for 3% of the time, Pallas kernels for 0%

commit v1 on v0

v1 whole, which is shorter than its diff:
```python
import functools

import jax
import jax.numpy as jnp
from jax import lax
from jax.experimental import pallas as pl
from jax.experimental.pallas import tpu as pltpu
from jax.sharding import PartitionSpec as P

STEPS = 2
SHARP = 7.0
STEP_RATE = 0.025
MESH = pl.DeviceIdType.MESH
NT = (((1,), (1,)), ((), ()))


def kernel(
    n, idx_ref, noise_ref, refs_hbm, out_ref,
    refs, gath, sib_out, sib_in, ring_out, ring_in, part, paths, base,
    sq_acc, scores, gram, weightb, totals_out, totals_in,
    load_sem, ag_send, ag_recv, agsib_send, agsib_recv,
    rs_send, rs_recv, rssib_send, rssib_recv, ex_send, ex_recv,
):
    chips, half = n // 2, n // 4
    m, width = noise_ref.shape
    rows = refs.shape[0]
    mh = m // 2
    all_refs = rows * n
    me = lax.axis_index("ref")
    chip, core = me // 2, me % 2
    other = 1 - core

    if n == 16:
        ring = chip // 2 + (chip % 2) * (chips - 1 - 2 * (chip // 2))

        def chip_at(r):
            back = r // half
            return back * (2 * (chips - 1 - r) + 1) + (1 - back) * 2 * r
    else:
        ring = chip

        def chip_at(r):
            return r

    def at(r):
        return (r + chips) % chips

    def pos(r, c):
        return chip_at(r) * 2 + c

    right = pos(at(ring + 1), core)
    left = pos(at(ring - 1), core)
    sibling = chip * 2 + other
    toward = (right, left)

    def columns(r, c):
        return pl.multiple_of(pos(r, c) * width, width)

    def remote(src, dst, send, recv, dev):
        return pltpu.make_async_remote_copy(
            src_ref=src, dst_ref=dst, send_sem=send, recv_sem=recv,
            device_id={"ref": dev}, device_id_type=MESH,
        )

    def load(r, c):
        cols = pl.ds(columns(r, c), width)
        return pltpu.make_async_copy(
            refs_hbm.at[:, cols], refs.at[:, cols], load_sem.at[r * 2 + c]
        )

    stages = [half] + list(range(half - 1, 0, -1)) + [0]

    def targets(k):
        if k == 0 or k == half:
            return [at(ring + k)]
        return [at(ring + k), at(ring - k)]

    for k in stages:
        for t in targets(k):
            load(t, other).start()
            load(t, core).start()

    barrier = pltpu.get_barrier_semaphore()

    def greet(i, carry):
        pl.semaphore_signal(
            barrier, inc=1, device_id={"ref": (me + i) % n}, device_id_type=MESH
        )
        return carry

    lax.fori_loop(1, n, greet, 0)

    offset = idx_ref[...] - me * rows
    lanes = lax.broadcasted_iota(jnp.int32, (m, rows), 1)
    weightb[...] = (lanes == offset).astype(jnp.float32).astype(jnp.bfloat16)
    sq_acc[...] = jnp.zeros_like(sq_acc)
    eye = (
        lax.broadcasted_iota(jnp.int32, (m, m), 0) == lax.broadcasted_iota(jnp.int32, (m, m), 1)
    ).astype(jnp.float32)
    pl.semaphore_wait(barrier, n - 1)

    def partial(r, c):
        cols = pl.ds(columns(r, c), width)
        return jnp.dot(weightb[...], refs[:, cols], preferred_element_type=jnp.float32)

    def squares(r, c):
        start = columns(r, c)
        chunk = 64

        def body(i, carry):
            rs = pl.ds(pl.multiple_of(i * chunk, chunk), chunk)
            total = sq_acc[rs, :]
            for j in range(width // 128):
                x = refs[rs, pl.ds(pl.multiple_of(start + j * 128, 128), 128)].astype(jnp.float32)
                total = total + x * x
            sq_acc[rs, :] = total
            return carry

        lax.fori_loop(0, rows // chunk, body, 0)

    def rs_copy(d, p, k):
        piece = pl.ds(p * mh, mh)
        return remote(
            ring_out.at[d, k - 1, piece, :], ring_in.at[d, k - 1, piece, :],
            rs_send.at[d, p, k - 1], rs_recv.at[d, p, k - 1], toward[d],
        )

    def rs_sib(t):
        return remote(
            sib_out.at[t], sib_in.at[t], rssib_send.at[t], rssib_recv.at[t], sibling
        )

    def has(d, p, k):
        return 1 <= k < half or (k == half and d == p)

    def reduce_scatter(first, tail):
        def compute(k):
            for t in targets(k):
                if first:
                    load(t, other).wait()
                sib_out[t] = partial(t, other).astype(jnp.bfloat16)
                rs_sib(t).start()
            for s, t in enumerate(targets(k)):
                if first:
                    load(t, core).wait()
                part[k % 2, s] = partial(t, core)

        compute(half)
        for k in range(half, 0, -1):
            ts = targets(k)
            for t in ts:
                rs_sib(t).wait_recv()
            for p in range(2):
                for d in range(2):
                    if not has(d, p, k):
                        continue
                    s = d if len(ts) == 2 else 0
                    piece = pl.ds(p * mh, mh)
                    value = part[k % 2, s, piece, :] + sib_in[ts[s], piece, :].astype(jnp.float32)
                    if has(d, p, k + 1):
                        rs_copy(d, p, k + 1).wait_recv()
                        value = value + ring_in[d, k, piece, :].astype(jnp.float32)
                    ring_out[d, k - 1, piece, :] = value.astype(jnp.bfloat16)
                    rs_copy(d, p, k).start()
            compute(k - 1)
            if first:
                for t in ts:
                    squares(t, other)
                    squares(t, core)
        if first:
            squares(ring, other)
            squares(ring, core)
        tail()
        rs_sib(ring).wait_recv()
        for p in range(2):
            for d in range(2):
                rs_copy(d, p, 1).wait_recv()
        total = part[0, 0] + sib_in[ring].astype(jnp.float32)
        for d in range(2):
            total = total + ring_in[d, 0].astype(jnp.float32)
        for k in stages:
            for t in targets(k):
                rs_sib(t).wait_send()
            for p in range(2):
                for d in range(2):
                    if has(d, p, k):
                        rs_copy(d, p, k).wait_send()
        return total

    def ex_copy(e, source, dev):
        return remote(
            totals_out.at[e], totals_in.at[e, source], ex_send.at[e, dev], ex_recv.at[e, source], dev
        )

    def exchange_start(e, row):
        totals_out[e] = jnp.broadcast_to(row, totals_out.shape[1:])

        def body(i, carry):
            ex_copy(e, me, (me + i) % n).start()
            return carry

        lax.fori_loop(1, n, body, 0)

    def exchange_wait(e):
        def body(i, total):
            source = (me + i) % n
            ex_copy(e, source, source).wait()
            return total + totals_in[e, source]

        return lax.fori_loop(1, n, body, totals_out[e])[0:1, :]

    def ag_copy(d, p, h, r):
        piece = gath.at[r, core, pl.ds(p * mh, mh), :]
        return remote(piece, piece, ag_send.at[d, p, h], ag_recv.at[d, p, h], toward[d])

    def ag_sib(r, c, p):
        piece = gath.at[r, c, pl.ds(p * mh, mh), :]
        return remote(piece, piece, agsib_send.at[r, p], agsib_recv.at[r, p], sibling)

    def ag_has(d, p, h):
        return 0 <= h < half - 1 or (h == half - 1 and d == p)

    def all_gather():
        gath[ring, core] = paths[...].astype(jnp.bfloat16)
        for p in range(2):
            for d in range(2):
                ag_copy(d, p, 0, ring).start()
        for p in range(2):
            ag_sib(ring, core, p).start()
        scores[...] = jnp.zeros_like(scores)
        gram[...] = jnp.zeros_like(gram)

        def multiply(r, c):
            block = gath[r, c]
            cols = pl.ds(columns(r, c), width)
            scores[...] += lax.dot_general(
                block, refs[:, cols], NT, preferred_element_type=jnp.float32
            )
            gram[...] += lax.dot_general(block, block, NT, preferred_element_type=jnp.float32)

        def multiply_all(k):
            for t in targets(k):
                multiply(t, core)
            for t in targets(k):
                for p in range(2):
                    ag_sib(t, other, p).wait_recv()
                multiply(t, other)

        for h in range(half):
            for p in range(2):
                for d in range(2):
                    if not ag_has(d, p, h):
                        continue
                    source = at(ring - 1 - h) if d == 0 else at(ring + 1 + h)
                    ag_copy(d, p, h, source).wait_recv()
                    if ag_has(d, p, h + 1):
                        ag_copy(d, p, h + 1, source).start()
                    ag_sib(source, core, p).start()
            multiply_all(h)
        multiply_all(half)
        for h in range(half):
            for p in range(2):
                for d in range(2):
                    if ag_has(d, p, h):
                        ag_copy(d, p, h, at(ring - h) if d == 0 else at(ring + h)).wait_send()
        for k in stages:
            for t in targets(k):
                for p in range(2):
                    ag_sib(t, core, p).wait_send()

    seeded = reduce_scatter(True, lambda: None)
    paths[...] = 0.6 * seeded + 0.8 * noise_ref[...]
    ref_sq = jnp.sum(sq_acc[...].T, axis=0, keepdims=True)
    exchange_start(0, jnp.broadcast_to(jnp.sum(ref_sq, axis=1, keepdims=True), (1, m)))
    sq_acc[0:8, :] = jnp.zeros((8, 128), jnp.float32)
    for j in range(rows // 128):
        sq_acc[j : j + 1, :] = ref_sq[:, j * 128 : (j + 1) * 128]

    def step(e, carry):
        all_gather()

        @pl.when(e == 1)
        def _():
            total = exchange_wait(0) / all_refs
            sq_acc[8:16, :] = jnp.broadcast_to(total, (8, 128))

        scale = sq_acc[8:9, 0:1]
        g = gram[...]
        diag = g * eye
        sq_col = jnp.sum(diag, axis=1, keepdims=True)
        sq_row = jnp.sum(diag, axis=0, keepdims=True)
        sums = jnp.zeros((m, 1), jnp.float32)
        for j in range(rows // 128):
            js = slice(j * 128, (j + 1) * 128)
            w = jnp.exp(
                SHARP
                * (2.0 * scale - sq_col - sq_acc[j : j + 1, :] + 2.0 * scores[:, js])
                / scale
            )
            sums = sums + jnp.sum(w, axis=1, keepdims=True)
            weightb[:, js] = w.astype(jnp.bfloat16)
        exchange_start(e, jnp.sum(eye * sums, axis=0, keepdims=True))

        def tail():
            mutual = jnp.exp(SHARP * (2.0 * scale - sq_col - sq_row + 2.0 * g) / scale) * (1.0 - eye)
            mutual_sum = jnp.sum(mutual, axis=1, keepdims=True)
            totals = jnp.sum(eye * exchange_wait(e), axis=1, keepdims=True)
            now = paths[...]
            pushed = jnp.dot(
                mutual, now, precision=lax.Precision.HIGHEST, preferred_element_type=jnp.float32
            )
            base[...] = (
                now
                + STEP_RATE / m * (mutual_sum * now - pushed)
                - STEP_RATE / all_refs * totals * now
            )

        pulled = reduce_scatter(False, tail)
        paths[...] = base[...] + STEP_RATE / all_refs * pulled
        return carry

    lax.fori_loop(1, STEPS + 1, step, 0)
    out_ref[...] = paths[...]


def shards(n, references, noise, init_idx):
    rows, depth = references.shape
    m, width = noise.shape
    chips, half = n // 2, n // 4
    dma = pltpu.SemaphoreType.DMA
    bf16, f32 = jnp.bfloat16, jnp.float32
    vmem = pl.BlockSpec(memory_space=pltpu.VMEM)
    flops = 2 * m * rows * depth * (2 * STEPS + 1)
    return pl.pallas_call(
        functools.partial(kernel, n),
        out_shape=jax.ShapeDtypeStruct((m, width), f32),
        in_specs=[vmem, vmem, pl.BlockSpec(memory_space=pl.ANY)],
        out_specs=vmem,
        scratch_shapes=[
            pltpu.VMEM((rows, depth), bf16),
            pltpu.VMEM((chips, 2, m, width), bf16),
            pltpu.VMEM((chips, m, width), bf16),
            pltpu.VMEM((chips, m, width), bf16),
            pltpu.VMEM((2, half, m, width), bf16),
            pltpu.VMEM((2, half, m, width), bf16),
            pltpu.VMEM((2, 2, m, width), f32),
            pltpu.VMEM((m, width), f32),
            pltpu.VMEM((m, width), f32),
            pltpu.VMEM((rows, 128), f32),
            pltpu.VMEM((m, rows), f32),
            pltpu.VMEM((m, m), f32),
            pltpu.VMEM((m, rows), bf16),
            pltpu.VMEM((STEPS + 1, 8, m), f32),
            pltpu.VMEM((STEPS + 1, n, 8, m), f32),
            dma((n,)),
            dma((2, 2, half)),
            dma((2, 2, half)),
            dma((chips, 2)),
            dma((chips, 2)),
            dma((2, 2, half)),
            dma((2, 2, half)),
            dma((chips,)),
            dma((chips,)),
            dma((STEPS + 1, n)),
            dma((STEPS + 1, n)),
        ],
        compiler_params=pltpu.CompilerParams(
            collective_id=0, has_side_effects=True, vmem_limit_bytes=56 * 1024 * 1024
        ),
        cost_estimate=pl.CostEstimate(
            flops=flops, bytes_accessed=2 * rows * depth, transcendentals=m * rows * STEPS
        ),
    )(init_idx.reshape(m, 1), noise, references)


def solution(mesh):
    in_specs = (P(("grp", "ref"), None), P("grp", "ref"), P("grp"))
    out_specs = P("grp", "ref")
    return jax.shard_map(
        functools.partial(shards, mesh.shape["ref"]),
        mesh=mesh, in_specs=in_specs, out_specs=out_specs, check_vma=False,
    )
```

time: 499 us -> 147 us (0.29)
  waiting for transfers between devices: 271 us -> 0 us
  Pallas kernels: 0 us -> 143 us
  blocking collectives: 94.7 us -> 0 us
  matrix products: 71.9 us -> 0 us
  other arithmetic: 24.2 us -> 0 us
  local copies, waits for them, and re-layouts: 22.7 us -> 3.27 us
  between operations: 14.4 us -> 0.01 us
    reduce_scatter x3 -> x0, waiting for transfers between devices: 220 us -> none  [the longest x2 144 us: shards(): lax.psum_scatter(lax.dot_general(references, weightb, (((0,), (1,)), ((),...]
    pallas_call x0 -> x1, Pallas kernels: none -> 143 us  [shards(): pl.pallas_call(functools.partial(kernel, n), out_shape=jax.ShapeDtypeStru...]
    psum x3 -> x0, blocking collectives: 94.7 us -> none  [the longest x2 63 us: shards(): totals = lax.psum(jnp.sum(weights, axis=1), 'ref')]
    dot_general x8 -> x0, matrix products: 71.9 us -> none  [the longest x2 29.9 us: shards(): lax.dot_general(references, weightb, (((0,), (1,)), ((), ())), preferred_...]
    all_gather x2 -> x0, waiting for transfers between devices: 50.8 us -> none  [shards(): piece = lax.all_gather(pathb, 'ref', axis=1, tiled=True)]
    gather x3 -> x0, local copies, waits for them, and re-layouts: 22.7 us -> none  [the longest x1 20.1 us: shards(): picked = references[jnp.clip(offset, 0, local_rows - 1)]]
    reduce_sum x3 -> x0, other arithmetic: 16.7 us -> none  [the longest x1 16.4 us: shards(): ref_sq = jnp.sum(jnp.square(references.astype(jnp.float32)), axis=1)]
    select_n x2 -> x0, other arithmetic: 5.11 us -> none  [the longest x1 4.45 us: shards(): picked = jnp.where(owned[:, None], picked, jnp.zeros_like(picked))]
  transfers between devices with their start and end apart: 5 -> 0, of which waited for: 5 -> 0; matrix products, arithmetic and copies ran while one was open for 3% -> 0% of each run, Pallas kernels for 0% -> 0%
where the time goes in v1:
time: 147 us
  Pallas kernels  143 us (97%)
  local copies, waits for them, and re-layouts  3.27 us (2%)
    pallas_call x1, Pallas kernels, shards(): pl.pallas_call(functools.partial(kernel, n), out_shape=jax.ShapeDtypeStru...  143 us

profile of v1, /device:TPU:0, one launch (start us, length us, event | category | flops | bytes accessed | tf_op | source)
XLA Modules:
  0.0 146.7 jit_solution(13190040515389506125)
XLA Ops:
  0.0 1.4 copy.4.idx_ref
  1.4 143.4 %shard_map.37 = f32[128,1024]{1,0:T(8,128)} custom-call(s32[128,1]{1,0:T(8,128)} %copy.4.idx_ref, f32[128,1024]{1,0:T(8,128)} %noise_ref.1, bf16[768,16384]{1,0:T(8,128)(2,1)} %refs_hbm.1), custom_call_target="tpu_custom_call" | custom-call | flops 16106127360 | bytes 25165824 | tf_op jit(solution)/shard_map/pallas_call | solution.py:334
  144.8 1.9 %copy.6 = f32[128,1024]{1,0:T(8,128)} copy(f32[128,1024]{1,0:T(8,128)} %shard_map.37) | data formatting | bytes 1048576

commit v2 on v1

--- a/solution.py
+++ b/solution.py
@@ -52,6 +52,7 @@
     left = pos(at(ring - 1), core)
     sibling = chip * 2 + other
     toward = (right, left)
+    order = ((0, 0), (1, 1), (0, 1), (1, 0))
 
     def columns(r, c):
         return pl.multiple_of(pos(r, c) * width, width)
@@ -75,11 +76,14 @@
             return [at(ring + k)]
         return [at(ring + k), at(ring - k)]
 
-    for k in stages:
+    def start_loads(k):
         for t in targets(k):
             load(t, other).start()
             load(t, core).start()
 
+    start_loads(half)
+    start_loads(half - 1)
+
     barrier = pltpu.get_barrier_semaphore()
 
     def greet(i, carry):
@@ -90,13 +94,14 @@
 
     lax.fori_loop(1, n, greet, 0)
 
-    offset = idx_ref[...] - me * rows
-    lanes = lax.broadcasted_iota(jnp.int32, (m, rows), 1)
-    weightb[...] = (lanes == offset).astype(jnp.float32).astype(jnp.bfloat16)
     sq_acc[...] = jnp.zeros_like(sq_acc)
     eye = (
         lax.broadcasted_iota(jnp.int32, (m, m), 0) == lax.broadcasted_iota(jnp.int32, (m, m), 1)
     ).astype(jnp.float32)
+    offset = jnp.broadcast_to(idx_ref[...] - me * rows, (m, m)).astype(jnp.float32)
+    offset = jnp.sum(eye * offset, axis=1, keepdims=True)
+    lanes = lax.broadcasted_iota(jnp.int32, (m, rows), 1).astype(jnp.float32)
+    weightb[...] = (lanes == offset).astype(jnp.float32).astype(jnp.bfloat16)
     pl.semaphore_wait(barrier, n - 1)
 
     def partial(r, c):
@@ -133,7 +138,7 @@
     def has(d, p, k):
         return 1 <= k < half or (k == half and d == p)
 
-    def reduce_scatter(first, tail):
+    def reduce_scatter(first, head, tail):
         def compute(k):
             for t in targets(k):
                 if first:
@@ -150,18 +155,21 @@
             ts = targets(k)
             for t in ts:
                 rs_sib(t).wait_recv()
-            for p in range(2):
-                for d in range(2):
-                    if not has(d, p, k):
-                        continue
-                    s = d if len(ts) == 2 else 0
-                    piece = pl.ds(p * mh, mh)
-                    value = part[k % 2, s, piece, :] + sib_in[ts[s], piece, :].astype(jnp.float32)
-                    if has(d, p, k + 1):
-                        rs_copy(d, p, k + 1).wait_recv()
-                        value = value + ring_in[d, k, piece, :].astype(jnp.float32)
-                    ring_out[d, k - 1, piece, :] = value.astype(jnp.bfloat16)
-                    rs_copy(d, p, k).start()
+            for d, p in order[2:] + order[:2]:
+                if not has(d, p, k):
+                    continue
+                s = d if len(ts) == 2 else 0
+                piece = pl.ds(p * mh, mh)
+                value = part[k % 2, s, piece, :] + sib_in[ts[s], piece, :].astype(jnp.float32)
+                if has(d, p, k + 1):
+                    rs_copy(d, p, k + 1).wait_recv()
+                    value = value + ring_in[d, k, piece, :].astype(jnp.float32)
+                ring_out[d, k - 1, piece, :] = value.astype(jnp.bfloat16)
+                rs_copy(d, p, k).start()
+            if first and k >= 2:
+                start_loads(k - 2)
+            if k == half:
+                head()
             compute(k - 1)
             if first:
                 for t in ts:
@@ -220,11 +228,10 @@
     def ag_has(d, p, h):
         return 0 <= h < half - 1 or (h == half - 1 and d == p)
 
-    def all_gather():
+    def all_gather(before_last):
         gath[ring, core] = paths[...].astype(jnp.bfloat16)
-        for p in range(2):
-            for d in range(2):
-                ag_copy(d, p, 0, ring).start()
+        for d, p in order:
+            ag_copy(d, p, 0, ring).start()
         for p in range(2):
             ag_sib(ring, core, p).start()
         scores[...] = jnp.zeros_like(scores)
@@ -247,16 +254,17 @@
                 multiply(t, other)
 
         for h in range(half):
-            for p in range(2):
-                for d in range(2):
-                    if not ag_has(d, p, h):
-                        continue
-                    source = at(ring - 1 - h) if d == 0 else at(ring + 1 + h)
-                    ag_copy(d, p, h, source).wait_recv()
-                    if ag_has(d, p, h + 1):
-                        ag_copy(d, p, h + 1, source).start()
-                    ag_sib(source, core, p).start()
             multiply_all(h)
+            if h == half - 1:
+                before_last()
+            for d, p in order:
+                if not ag_has(d, p, h):
+                    continue
+                source = at(ring - 1 - h) if d == 0 else at(ring + 1 + h)
+                ag_copy(d, p, h, source).wait_recv()
+                if ag_has(d, p, h + 1):
+                    ag_copy(d, p, h + 1, source).start()
+                ag_sib(source, core, p).start()
         multiply_all(half)
         for h in range(half):
             for p in range(2):
@@ -268,7 +276,7 @@
                 for p in range(2):
                     ag_sib(t, core, p).wait_send()
 
-    seeded = reduce_scatter(True, lambda: None)
+    seeded = reduce_scatter(True, lambda: None, lambda: None)
     paths[...] = 0.6 * seeded + 0.8 * noise_ref[...]
     ref_sq = jnp.sum(sq_acc[...].T, axis=0, keepdims=True)
     exchange_start(0, jnp.broadcast_to(jnp.sum(ref_sq, axis=1, keepdims=True), (1, m)))
@@ -277,12 +285,13 @@
         sq_acc[j : j + 1, :] = ref_sq[:, j * 128 : (j + 1) * 128]
 
     def step(e, carry):
-        all_gather()
-
-        @pl.when(e == 1)
-        def _():
-            total = exchange_wait(0) / all_refs
-            sq_acc[8:16, :] = jnp.broadcast_to(total, (8, 128))
+        def before_last():
+            @pl.when(e == 1)
+            def _():
+                total = exchange_wait(0) / all_refs
+                sq_acc[8:16, :] = jnp.broadcast_to(total, (8, 128))
+
+        all_gather(before_last)
 
         scale = sq_acc[8:9, 0:1]
         g = gram[...]
@@ -299,7 +308,9 @@
             )
             sums = sums + jnp.sum(w, axis=1, keepdims=True)
             weightb[:, js] = w.astype(jnp.bfloat16)
-        exchange_start(e, jnp.sum(eye * sums, axis=0, keepdims=True))
+
+        def head():
+            exchange_start(e, jnp.sum(eye * sums, axis=0, keepdims=True))
 
         def tail():
             mutual = jnp.exp(SHARP * (2.0 * scale - sq_col - sq_row + 2.0 * g) / scale) * (1.0 - eye)
@@ -315,7 +326,7 @@
                 - STEP_RATE / all_refs * totals * now
             )
 
-        pulled = reduce_scatter(False, tail)
+        pulled = reduce_scatter(False, head, tail)
         paths[...] = base[...] + STEP_RATE / all_refs * pulled
         return carry
 
@@ -370,7 +381,7 @@
         cost_estimate=pl.CostEstimate(
             flops=flops, bytes_accessed=2 * rows * depth, transcendentals=m * rows * STEPS
         ),
-    )(init_idx.reshape(m, 1), noise, references)
+    )(init_idx.reshape(1, m), noise, references)
 
 
 def solution(mesh):

time: 147 us -> 135 us (0.918)
  Pallas kernels: 143 us -> 133 us
    pallas_call x1, Pallas kernels: 143 us -> 133 us  [shards(): pl.pallas_call(functools.partial(kernel, n), out_shape=jax.ShapeDtypeStru...]
where the time goes in v2:
time: 135 us
  Pallas kernels  133 us (99%)
  local copies, waits for them, and re-layouts  1.89 us (1%)
    pallas_call x1, Pallas kernels, shards(): pl.pallas_call(functools.partial(kernel, n), out_shape=jax.ShapeDtypeStru...  133 us

profile of v2, /device:TPU:0, one launch (start us, length us, event | category | flops | bytes accessed | tf_op | source)
XLA Modules:
  0.0 135.1 jit_solution(5350017572262325353)
XLA Ops:
  0.0 133.2 %shard_map.37 = f32[128,1024]{1,0:T(8,128)} custom-call(s32[1,128]{1,0:T(1,128)} %bitcast.1, f32[128,1024]{1,0:T(8,128)} %noise_ref.1, bf16[768,16384]{1,0:T(8,128)(2,1)} %refs_hbm.1), custom_call_target="tpu_custom_call" | custom-call | flops 16106127360 | bytes 25165824 | tf_op jit(solution)/shard_map/pallas_call | solution.py:345
  133.2 1.9 %copy.5 = f32[128,1024]{1,0:T(8,128)} copy(f32[128,1024]{1,0:T(8,128)} %shard_map.37) | data formatting | bytes 1048576
